TPU v7x, 32 devices: a whole 2x2x4 slice. The times are simulated.
32 devices in a mesh: section: 4 (over z), dp: 2 (over y), tensor: 4 (over x, core).
Axes of the slice: x: 2, y: 2, z: 4, core: 2. Of those that a mesh axis runs over, the one named last changes fastest.
Arguments:
- context: bfloat16 [4, 1024, 8192], P('section', 'dp', 'tensor'), may hold values from -6 to 6
- residual: bfloat16 [4, 1024, 8192], P('section', 'tensor', 'dp')
- out_weight: bfloat16 [4, 8192, 8192], P('section', 'tensor', 'dp'), may hold values from -0.0625 to 0.0625
- norm_gain: float32 [4, 8192], P('section'), may hold values from 0.25 to 1.75
- valid_tokens: int32 [4], P('section'), may hold values from 512 to 1024, as said below
Outputs:
- normed: bfloat16 [4, 1024, 8192], P('section', 'tensor', 'dp')
- handoff: bfloat16 [4, 1024, 8192], P('section', 'tensor', 'dp')
Inputs may be any that keep to these rules, and one draw needn't show every extreme that they name: `valid_tokens`: some section's micro-batch is full in every draw.
All inputs are finite; a program needn't handle non-finite values.
Results may differ from a plain program's by a relative error of at most 0.018.
Values may be sent and summed in bfloat16 or wider, within the bound.
A program may use at most 64 MiB of HBM per device.

v0:
```python
import jax
import jax.numpy as jnp
from jax import lax
from jax.sharding import PartitionSpec as P


def passed_along(value, axis, steps):
    count = lax.axis_size(axis)
    leading, last = (max(0, -steps), min(count, count - steps))
    return lax.ppermute(value, axis, [(source, source + steps) for source in range(leading, last)])


def on_device(context, residual, out_weight, norm_gain, valid_tokens):
    whole = lax.all_gather(context[0], "dp", axis=0, tiled=True)
    weight = out_weight[0]
    rows_here = residual.shape[1]
    tensor_pos = lax.axis_index("tensor")
    attn = lax.psum_scatter(
        jnp.dot(whole, weight, preferred_element_type=jnp.float32).astype(jnp.bfloat16),
        "tensor",
        scatter_dimension=0,
        tiled=True,
    ).astype(jnp.float32)
    hidden = residual[0].astype(jnp.float32) + attn
    full_rows = lax.all_to_all(
        hidden.astype(jnp.bfloat16), "dp", split_axis=0, concat_axis=1, tiled=True
    ).astype(hidden.dtype)
    mean_sq = jnp.mean(full_rows * full_rows, axis=1, keepdims=True)
    scaled = (full_rows * lax.rsqrt(mean_sq + 1e-06) * norm_gain[0][None, :]).astype(jnp.bfloat16)
    normed = lax.all_to_all(scaled, "dp", split_axis=1, concat_axis=0, tiled=True)
    row_ids = tensor_pos * rows_here + jnp.arange(rows_here, dtype=jnp.int32)
    keep = (row_ids < valid_tokens[0])[:, None]
    normed = jnp.where(keep, normed, jnp.zeros_like(normed))
    outgoing = jnp.where(keep, hidden, 0.0).astype(jnp.bfloat16)
    handoff = passed_along(outgoing, "section", 1)
    return (normed[None], handoff[None])


def solution(mesh):
    placed = (
        P("section", "dp", "tensor"),
        P("section", "tensor", "dp"),
        P("section", "tensor", "dp"),
        P("section", None),
        P("section"),
    )
    return jax.shard_map(
        on_device,
        mesh=mesh,
        in_specs=placed,
        out_specs=(P("section", "tensor", "dp"), P("section", "tensor", "dp")),
        check_vma=False,
    )
```

profile of v0, /device:TPU:0, one launch (start us, length us, event | category | flops | bytes accessed | tf_op | source)
XLA Modules:
  0.0 239.6 jit_solution(2153378044570168318)
XLA Ops:
  7.2 0.0 all-gather.3.cloned.1.call-start
  7.2 0.7 all-gather.3.cloned.1.call-update
  7.9 0.0 reduce-scatter.2.cloned.1.call-start
  7.9 61.1 %all-gather.3.cloned.1.call-done = bf16[1,1024,2048]{2,1,0:T(8,128)(2,1)} async-done(((bf16[1,512,2048]{2,1,0:T(8,128)(2,1)}), bf16[1,1024,2048]{2,1,0:T(8,128)(2,1)}) %all-gather.3.cloned.1.call-update) | async-done | bytes 4194320 | tf_op jit(solution)/shard_map/all_gather | solution.py:14
  69.0 22.9 %fusion.2 = bf16[1024,4096]{1,0:T(8,128)(2,1)} fusion(bf16[1,2048,4096]{2,1,0:T(8,128)(2,1)} %param.7, bf16[1,1024,2048]{2,1,0:T(8,128)(2,1)} %all-gather.3.cloned.1.call-done), kind=kOutput, calls=%fused_computation.2 | convolution fusion | flops 17184063488 | bytes 29360128 | tf_op jit(solution)/shard_map/dot_general | solution.py:19
  91.9 0.0 copy-start
  91.9 0.0 reduce-scatter.2.cloned.1.call-update
  92.8 71.1 %reduce-scatter.2.cloned.1.call-done = bf16[256,4096]{1,0:T(8,128)(2,1)} async-done(((bf16[1024,4096]{1,0:T(8,128)(2,1)}), bf16[256,4096]{1,0:T(8,128)(2,1)}) %reduce-scatter.2.cloned.1.call-update) | async-done | bytes 2097168 | tf_op jit(solution)/shard_map/reduce_scatter | solution.py:18
  163.8 0.0 copy-done
  163.8 4.7 %select_convert_fusion = (bf16[256,4096]{1,0:T(8,128)(2,1)}, bf16[256,4096]{1,0:T(8,128)(2,1)}) fusion(bf16[256,4096]{1,0:T(8,128)(2,1)} %reduce-scatter.2.cloned.1.call-done, bf16[1,256,4096]{2,1,0:T(8,128)(2,1)S(1)} %copy-done, pred[256]{0:T(512)(128)(4,1)S(1)} %add_compare_fusion), kind=kLoop, calls=%fused_computation.10 | loop fusion | flops 6291456 | bytes 8388864 | tf_op jit(solution)/shard_map/convert_element_type | solution.py:34
  168.5 0.0 copy-start.1
  168.5 3.9 %all-to-all-start = ((bf16[2,128,4096]{2,1,0:T(8,128)(2,1)}), bf16[2,128,4096]{2,1,0:T(8,128)(2,1)S(1)}, u32[]{:S(2)}, u32[]{:S(2)}) async-start(bf16[2,128,4096]{2,1,0:T(8,128)(2,1)} %bitcast.22), calls=%async_computation.1 | async-start | bytes 4194304 | tf_op jit(solution)/shard_map/all_to_all | solution.py:25
  172.4 0.5 broadcast.52
  172.9 0.0 copy-done.1
  172.9 0.6 reduce.5
  173.6 4.7 %collective-permute-start = (bf16[256,4096]{1,0:T(8,128)(2,1)}, bf16[256,4096]{1,0:T(8,128)(2,1)}, u32[]{:S(2)}, u32[]{:S(2)}) collective-permute-start(bf16[256,4096]{1,0:T(8,128)(2,1)} %get-tuple-element.2), channel_id=1, source_target_pairs={{0,8},{8,16},{16,24},{1,9},{9,17},{17,25},{2,10},{10,18},{18,26},{... | collective-permute-start | bytes 6291464 | tf_op jit(solution)/shard_map/ppermute | solution.py:10
  178.3 19.2 %all-to-all-done = bf16[2,128,4096]{2,1,0:T(8,128)(2,1)S(1)} async-done(((bf16[2,128,4096]{2,1,0:T(8,128)(2,1)}), bf16[2,128,4096]{2,1,0:T(8,128)(2,1)S(1)}, u32[]{:S(2)}, u32[]{:S(2)}) %all-to-all-start) | async-done | bytes 2097184 | tf_op jit(solution)/shard_map/all_to_all | solution.py:25
  197.5 0.5 fusion.5
  198.0 1.9 fusion.10
  199.9 3.8 %all-to-all-start.1 = ((bf16[128,2,4096]{2,0,1:T(8,128)(2,1)}), bf16[128,2,4096]{2,0,1:T(8,128)(2,1)S(1)}, u32[]{:S(2)}, u32[]{:S(2)}) async-start(bf16[128,2,4096]{2,0,1:T(8,128)(2,1)} %fusion.10), calls=%async_computation.2 | async-start | bytes 4194304 | tf_op jit(solution)/shard_map/all_to_all | solution.py:30
  203.7 18.5 %collective-permute-done = bf16[256,4096]{1,0:T(8,128)(2,1)} collective-permute-done((bf16[256,4096]{1,0:T(8,128)(2,1)}, bf16[256,4096]{1,0:T(8,128)(2,1)}, u32[]{:S(2)}, u32[]{:S(2)}) %collective-permute-start) | collective-permute-done | bytes 2097184 | tf_op jit(solution)/shard_map/ppermute | solution.py:10
  222.2 5.8 %all-to-all-done.1 = bf16[128,2,4096]{2,0,1:T(8,128)(2,1)S(1)} async-done(((bf16[128,2,4096]{2,0,1:T(8,128)(2,1)}), bf16[128,2,4096]{2,0,1:T(8,128)(2,1)S(1)}, u32[]{:S(2)}, u32[]{:S(2)}) %all-to-all-start.1) | async-done | bytes 2097184 | tf_op jit(solution)/shard_map/all_to_all | solution.py:30
  227.9 1.7 bitcast_select_fusion
  229.6 3.1 %copy.9 = bf16[1,256,4096]{2,1,0:T(8,128)(2,1)} copy(bf16[1,256,4096]{2,1,0:T(8,128)(2,1)} %bitcast.8) | data formatting | bytes 4194304
  (3 shorter events, 0.0 us)
Async XLA Ops:
  7.2 61.9 %all-gather.3.cloned.1.call-start = ((), (), s32[]{:S(2)}) async-start(), calls=%async_computation.4 | async-start | bytes 6291456 | tf_op jit(solution)/shard_map/all_gather | solution.py:14
  7.9 155.9 %reduce-scatter.2.cloned.1.call-start = ((), (), s32[]{:S(2)}) async-start(), calls=%async_computation.3 | async-start | bytes 10485760 | tf_op jit(solution)/shard_map/reduce_scatter | solution.py:18
  91.9 71.9 %copy-start = (bf16[1,256,4096]{2,1,0:T(8,128)(2,1)S(1)}, bf16[1,256,4096]{2,1,0:T(8,128)(2,1)}, u32[]{:S(2)}) copy-start(bf16[1,256,4096]{2,1,0:T(8,128)(2,1)} %param.6) | copy-start | bytes 6291460
  168.5 4.4 %copy-start.1 = (f32[1,8192]{1,0:T(1,128)S(1)}, f32[1,8192]{1,0:T(1,128)}, u32[]{:S(2)}) copy-start(f32[1,8192]{1,0:T(1,128)} %param.8) | copy-start | bytes 98308
  168.5 29.0 %all-to-all-start = ((bf16[2,128,4096]{2,1,0:T(8,128)(2,1)}), bf16[2,128,4096]{2,1,0:T(8,128)(2,1)S(1)}, u32[]{:S(2)}, u32[]{:S(2)}) async-start(bf16[2,128,4096]{2,1,0:T(8,128)(2,1)} %bitcast.22), calls=%async_computation.1 | async-start | bytes 4194304 | tf_op jit(solution)/shard_map/all_to_all | solution.py:25
  173.6 48.6 %collective-permute-start = (bf16[256,4096]{1,0:T(8,128)(2,1)}, bf16[256,4096]{1,0:T(8,128)(2,1)}, u32[]{:S(2)}, u32[]{:S(2)}) collective-permute-start(bf16[256,4096]{1,0:T(8,128)(2,1)} %get-tuple-element.2), channel_id=1, source_target_pairs={{0,8},{8,16},{16,24},{1,9},{9,17},{17,25},{2,10},{10,18},{18,26},{... | collective-permute-start | bytes 6291464 | tf_op jit(solution)/shard_map/ppermute | solution.py:10
  199.9 28.0 %all-to-all-start.1 = ((bf16[128,2,4096]{2,0,1:T(8,128)(2,1)}), bf16[128,2,4096]{2,0,1:T(8,128)(2,1)S(1)}, u32[]{:S(2)}, u32[]{:S(2)}) async-start(bf16[128,2,4096]{2,0,1:T(8,128)(2,1)} %fusion.10), calls=%async_computation.2 | async-start | bytes 4194304 | tf_op jit(solution)/shard_map/all_to_all | solution.py:30
Sparse Core Ops, SparseCore 0:
  9.5 59.4 all-gather.2
  92.1 71.7 reduce-scatter.1
where the time goes:
time: 240 us
  waiting for transfers between devices  176 us (73%)
  matrix products  22.9 us (10%)
  between operations  14.9 us (6%)
  starting transfers between devices  12.5 us (5%)
  other arithmetic  9.44 us (4%)
  local copies, waits for them, and re-layouts  3.66 us (2%)
    reduce_scatter x1, waiting for transfers between devices, on_device(): lax.psum_scatter(jnp.dot(whole, weight, preferred_element_type=jnp.float3...  71.1 us
    all_gather x1, waiting for transfers between devices, on_device(): whole = lax.all_gather(context[0], 'dp', axis=0, tiled=True)  61.1 us
    dot_general x1, matrix products, on_device(): jnp.dot(whole, weight, preferred_element_type=jnp.float32)  22.9 us
    all_to_all x1, waiting for transfers between devices, on_device(): lax.all_to_all(hidden.astype(jnp.bfloat16), 'dp', split_axis=0, concat_ax...  19.2 us
    ppermute x1, waiting for transfers between devices, passed_along(): lax.ppermute(value, axis, [(source, source + steps) for source in range(l...  18.5 us
    all_to_all x1, waiting for transfers between devices, on_device(): lax.all_to_all(scaled, 'dp', split_axis=1, concat_axis=0, tiled=True)  5.76 us
  transfers between devices with their start and end apart: 5, of which 5 were waited for; matrix products, arithmetic and copies ran while one was open for 2% of the time, Pallas kernels for 0%

commit v1 on v0

v1 whole, which is shorter than its diff:
```python
import functools

import jax
import jax.numpy as jnp
from jax import lax
from jax.experimental import pallas as pl
from jax.experimental.pallas import tpu as pltpu
from jax.sharding import PartitionSpec as P

MESH = pl.DeviceIdType.MESH
PIECES = 8
AHEAD = 2
LAG = 2


def relay_kernel(
    sizes, valid_ref, context, residual, weight, gain, normed, handoff,
    rows_all, held_w, held_res, mine, pair_out, pair_in, chip_out, chip_in,
    hidden, passed, scaled, sq_out, sq_in,
    ctx_sem, w_sem, res_sem, y_send, y_recv, pair_send, pair_recv,
    chip_send, chip_recv, z_send, z_recv, sq_send, sq_recv, out_sem, zero_sem,
):
    sections, dps, chips, blocks, rows, depth, cols, r, steps, tile = sizes
    tiles = cols // tile
    sec = lax.axis_index("section")
    dp = lax.axis_index("dp")
    tensor = lax.axis_index("tensor")
    core = lax.rem(tensor, 2)
    chip = lax.div(tensor, 2)
    sibling = tensor + 1 - 2 * core
    dp_at = [lax.rem(dp + j, dps) for j in range(1, dps)]
    chip_at = [lax.rem(chip + j, chips) for j in range(1, chips)]

    def span(k):
        return pl.ds(pl.multiple_of(k * r, r), r)

    own = pl.ds(dp * blocks, blocks)
    ctx_load = pltpu.make_async_copy(context, rows_all.at[own], ctx_sem)
    ctx_load.start()

    def w_load(n):
        at = pl.ds(pl.multiple_of(n * tile, tile), tile)
        return pltpu.make_async_copy(weight.at[:, at], held_w.at[:, at], w_sem.at[n])

    def w_start(n, carry):
        w_load(n).start()
        return carry

    lax.fori_loop(0, tiles, w_start, 0)
    res_load = pltpu.make_async_copy(residual, held_res, res_sem)
    res_load.start()

    barrier = pltpu.get_barrier_semaphore()
    for d in dp_at:
        pl.semaphore_signal(barrier, inc=1, device_id={"dp": d}, device_id_type=MESH)
    pl.semaphore_signal(barrier, inc=1, device_id={"tensor": sibling}, device_id_type=MESH)
    for q in chip_at:
        pl.semaphore_signal(barrier, inc=1, device_id={"tensor": q * 2 + core}, device_id_type=MESH)

    @pl.when(sec > 0)
    def _():
        pl.semaphore_signal(barrier, inc=1, device_id={"section": sec - 1}, device_id_type=MESH)

    @pl.when(sec < sections - 1)
    def _():
        pl.semaphore_signal(barrier, inc=1, device_id={"section": sec + 1}, device_id_type=MESH)

    inner = (sec > 0) & (sec < sections - 1)

    @pl.when(inner)
    def _():
        pl.semaphore_wait(barrier, dps + chips + 1)

    @pl.when(jnp.logical_not(inner))
    def _():
        pl.semaphore_wait(barrier, dps + chips)

    def y_copy(k, j):
        return pltpu.make_async_remote_copy(
            src_ref=context.at[:, :, span(k), :],
            dst_ref=rows_all.at[own, :, span(k), :],
            send_sem=y_send.at[k, j],
            recv_sem=y_recv.at[k, j],
            device_id={"dp": dp_at[j]},
            device_id_type=MESH,
        )

    def pair_copy(k):
        return pltpu.make_async_remote_copy(
            src_ref=pair_out.at[k],
            dst_ref=pair_in.at[k],
            send_sem=pair_send.at[k],
            recv_sem=pair_recv.at[k],
            device_id={"tensor": sibling},
            device_id_type=MESH,
        )

    def chip_copy(k, j):
        return pltpu.make_async_remote_copy(
            src_ref=chip_out.at[j, span(k), :],
            dst_ref=chip_in.at[j, span(k), :],
            send_sem=chip_send.at[k, j],
            recv_sem=chip_recv.at[k, j],
            device_id={"tensor": chip_at[j] * 2 + core},
            device_id_type=MESH,
        )

    def z_copy(k):
        return pltpu.make_async_remote_copy(
            src_ref=passed.at[span(k), :],
            dst_ref=handoff.at[span(k), :],
            send_sem=z_send.at[k],
            recv_sem=z_recv.at[k],
            device_id={"section": lax.rem(sec + 1, sections)},
            device_id_type=MESH,
        )

    def sq_copy(k, j):
        return pltpu.make_async_remote_copy(
            src_ref=sq_out.at[k],
            dst_ref=sq_in.at[j, k],
            send_sem=sq_send.at[k, j],
            recv_sem=sq_recv.at[k, j],
            device_id={"dp": dp_at[j]},
            device_id_type=MESH,
        )

    def out_copy(k):
        return pltpu.make_async_copy(
            scaled.at[span(k), :], normed.at[span(k), :], out_sem.at[k]
        )

    def zero_copy(k):
        return pltpu.make_async_copy(
            passed.at[span(0), :], handoff.at[span(k), :], zero_sem.at[k]
        )

    for k in range(min(AHEAD, steps)):
        for j in range(dps - 1):
            y_copy(k, j).start()

    @pl.when(sec == 0)
    def _():
        passed[span(0), :] = jnp.zeros((r, cols), passed.dtype)

        def begin(k, carry):
            zero_copy(k).start()
            return carry

        def finish(k, carry):
            zero_copy(k).wait()
            return carry

        lax.fori_loop(0, steps, begin, 0)
        lax.fori_loop(0, steps, finish, 0)

    ctx_load.wait()
    half = chips * r

    def product(k):
        for j in range(dps - 1):
            y_copy(k, j).wait_recv()

        @pl.when(k + AHEAD < steps)
        def _():
            for j in range(dps - 1):
                y_copy(k + AHEAD, j).start()

        def one_tile(n, carry):
            @pl.when(k == 0)
            def _():
                w_load(n).wait()

            at = pl.ds(pl.multiple_of(n * tile, tile), tile)
            lhs = jnp.concatenate(
                [rows_all[:, 1 - core, span(k), :], rows_all[:, core, span(k), :]], axis=0
            ).reshape(2 * half, depth)
            part = jnp.dot(lhs, held_w[:, at], preferred_element_type=jnp.float32)
            pair_out[k, :, :, at] = part[:half].astype(jnp.bfloat16).reshape(chips, r, tile)
            mine[:, :, at] = part[half:].reshape(chips, r, tile)
            return carry

        lax.fori_loop(0, tiles, one_tile, 0)
        pair_copy(k).start()

    def combine(k):
        pair_copy(k).wait_recv()
        for j in range(chips - 1):
            both = mine[chip_at[j]] + pair_in[k, chip_at[j]].astype(jnp.float32)
            chip_out[j, span(k), :] = both.astype(jnp.bfloat16)
            chip_copy(k, j).start()
        both = mine[chip] + pair_in[k, chip].astype(jnp.float32)
        hidden[span(k), :] = both

    def row_mask(k):
        ids = tensor * rows + k * r + lax.broadcasted_iota(jnp.int32, (r, 1), 0)
        return ids < valid_ref[0]

    def add_residual(k):
        @pl.when(k == 0)
        def _():
            res_load.wait()

        for j in range(chips - 1):
            chip_copy(k, j).wait_recv()
        keep = row_mask(k)
        total = jnp.zeros((r, 128), jnp.float32)
        for n in range(tiles):
            at = pl.ds(n * tile, tile)
            h = hidden[span(k), at]
            for j in range(chips - 1):
                h = h + chip_in[j, span(k), at].astype(jnp.float32)
            h = h + held_res[span(k), at].astype(jnp.float32)
            hidden[span(k), at] = h
            passed[span(k), at] = jnp.where(keep, h, 0.0).astype(jnp.bfloat16)
            sq = h * h
            for c in range(tile // 128):
                total = total + sq[:, c * 128 : (c + 1) * 128]
        sq_out[k] = total
        for j in range(dps - 1):
            sq_copy(k, j).start()

        @pl.when(sec < sections - 1)
        def _():
            z_copy(k).start()

    def normalize(k):
        total = sq_out[k]
        for j in range(dps - 1):
            sq_copy(k, j).wait_recv()
            total = total + sq_in[j, k]
        mean_sq = jnp.sum(total, axis=1, keepdims=True) / (dps * cols)
        scale = jnp.where(row_mask(k), lax.rsqrt(mean_sq + 1e-06), 0.0)
        for n in range(tiles):
            at = pl.ds(n * tile, tile)
            g = gain[:, pl.ds(pl.multiple_of(dp * cols + n * tile, tile), tile)]
            scaled[span(k), at] = (hidden[span(k), at] * scale * g).astype(jnp.bfloat16)
        out_copy(k).start()

    def step(s, carry):
        @pl.when(s < steps)
        def _():
            product(s)

        @pl.when(s > LAG)
        def _():
            normalize(s - LAG - 1)

        @pl.when(s < steps)
        def _():
            combine(s)

        @pl.when((s >= LAG) & (s < steps + LAG))
        def _():
            add_residual(s - LAG)

        return carry

    lax.fori_loop(0, steps + LAG + 1, step, 0)

    def drain(k, carry):
        for j in range(dps - 1):
            y_copy(k, j).wait_send()
            sq_copy(k, j).wait_send()
        pair_copy(k).wait_send()
        for j in range(chips - 1):
            chip_copy(k, j).wait_send()
        out_copy(k).wait()

        @pl.when(sec < sections - 1)
        def _():
            z_copy(k).wait_send()

        @pl.when(sec > 0)
        def _():
            z_copy(k).wait_recv()

        return carry

    lax.fori_loop(0, steps, drain, 0)


def on_device(context, residual, out_weight, norm_gain, valid_tokens):
    sections, dps, tensors = (lax.axis_size(a) for a in ("section", "dp", "tensor"))
    chips = tensors // 2
    rows, cols = residual.shape[1:]
    local, depth = context.shape[1:]
    blocks = local // (2 * rows)
    assert blocks * dps == chips
    r = max(16, rows // PIECES)
    steps = rows // r
    tile = min(512, cols)
    sizes = (sections, dps, chips, blocks, rows, depth, cols, r, steps, tile)
    bf16, f32 = jnp.bfloat16, jnp.float32
    dma = pltpu.SemaphoreType.DMA
    total_rows = local * dps
    anywhere = pl.BlockSpec(memory_space=pl.ANY)
    out = jax.ShapeDtypeStruct((rows, cols), bf16)
    normed, handoff = pl.pallas_call(
        functools.partial(relay_kernel, sizes),
        out_shape=(out, out),
        in_specs=[
            pl.BlockSpec(memory_space=pltpu.SMEM),
            anywhere,
            anywhere,
            anywhere,
            pl.BlockSpec(memory_space=pltpu.VMEM),
        ],
        out_specs=(anywhere, anywhere),
        scratch_shapes=[
            pltpu.VMEM((chips, 2, rows, depth), bf16),
            pltpu.VMEM((depth, cols), bf16),
            pltpu.VMEM((rows, cols), bf16),
            pltpu.VMEM((chips, r, cols), f32),
            pltpu.VMEM((steps, chips, r, cols), bf16),
            pltpu.VMEM((steps, chips, r, cols), bf16),
            pltpu.VMEM((chips - 1, rows, cols), bf16),
            pltpu.VMEM((chips - 1, rows, cols), bf16),
            pltpu.VMEM((rows, cols), f32),
            pltpu.VMEM((rows, cols), bf16),
            pltpu.VMEM((rows, cols), bf16),
            pltpu.VMEM((steps, r, 128), f32),
            pltpu.VMEM((dps - 1, steps, r, 128), f32),
            dma,
            dma((cols // tile,)),
            dma,
            dma((steps, dps - 1)),
            dma((steps, dps - 1)),
            dma((steps,)),
            dma((steps,)),
            dma((steps, chips - 1)),
            dma((steps, chips - 1)),
            dma((steps,)),
            dma((steps,)),
            dma((steps, dps - 1)),
            dma((steps, dps - 1)),
            dma((steps,)),
            dma((steps,)),
        ],
        compiler_params=pltpu.CompilerParams(
            collective_id=0, has_side_effects=True, vmem_limit_bytes=56 * 2**20
        ),
        cost_estimate=pl.CostEstimate(
            flops=2 * total_rows * depth * cols,
            bytes_accessed=2 * (depth * cols + local * depth + 3 * rows * cols),
            transcendentals=0,
        ),
        name="relay",
    )(
        valid_tokens,
        context.reshape(blocks, 2, rows, depth),
        residual[0],
        out_weight[0],
        norm_gain,
    )
    return (normed[None], handoff[None])


def solution(mesh):
    placed = (
        P("section", "dp", "tensor"),
        P("section", "tensor", "dp"),
        P("section", "tensor", "dp"),
        P("section", None),
        P("section"),
    )
    return jax.shard_map(
        on_device,
        mesh=mesh,
        in_specs=placed,
        out_specs=(P("section", "tensor", "dp"), P("section", "tensor", "dp")),
        check_vma=False,
    )
```

time: 240 us -> 83.6 us (0.35)
  waiting for transfers between devices: 176 us -> 0 us
  Pallas kernels: 0 us -> 77.5 us
  matrix products: 22.9 us -> 0 us
  between operations: 14.9 us -> 1.29 us
  starting transfers between devices: 12.5 us -> 0 us
  other arithmetic: 9.44 us -> 0 us
    pallas_call x0 -> x1, Pallas kernels: none -> 77.5 us  [on_device(): pl.pallas_call(functools.partial(relay_kernel, sizes), out_shape=(out, ou...]
    reduce_scatter x1 -> x0, waiting for transfers between devices: 71.1 us -> none  [on_device(): lax.psum_scatter(jnp.dot(whole, weight, preferred_element_type=jnp.float3...]
    all_gather x1 -> x0, waiting for transfers between devices: 61.1 us -> none  [on_device(): whole = lax.all_gather(context[0], 'dp', axis=0, tiled=True)]
    all_to_all x2 -> x0, waiting for transfers between devices: 24.9 us -> none  [the longest x1 19.2 us: on_device(): lax.all_to_all(hidden.astype(jnp.bfloat16), 'dp', split_axis=0, concat_ax...]
    dot_general x1 -> x0, matrix products: 22.9 us -> none  [on_device(): jnp.dot(whole, weight, preferred_element_type=jnp.float32)]
    ppermute x1 -> x0, waiting for transfers between devices: 18.5 us -> none  [passed_along(): lax.ppermute(value, axis, [(source, source + steps) for source in range(l...]
    all_to_all x2 -> x0, starting transfers between devices: 7.66 us -> none  [the longest x1 3.9 us: on_device(): lax.all_to_all(hidden.astype(jnp.bfloat16), 'dp', split_axis=0, concat_ax...]
    convert_element_type x2 -> x0, other arithmetic: 6.6 us -> none  [the longest x1 4.66 us: on_device(): outgoing = jnp.where(keep, hidden, 0.0).astype(jnp.bfloat16)]
  transfers between devices with their start and end apart: 5 -> 0, of which waited for: 5 -> 0; matrix products, arithmetic and copies ran while one was open for 2% -> 0% of each run, Pallas kernels for 0% -> 0%
where the time goes in v1:
time: 83.6 us; the launch traced here: 83.4 us
  Pallas kernels  77.5 us (93%)
  local copies, waits for them, and re-layouts  4.6 us (6%)
  between operations  1.29 us (2%)
    pallas_call x1, Pallas kernels, on_device(): pl.pallas_call(functools.partial(relay_kernel, sizes), out_shape=(out, ou...  77.5 us
    unnamed x4, local copies, waits for them, and re-layouts  4.6 us

profile of v1, /device:TPU:0, one launch (start us, length us, event | category | flops | bytes accessed | tf_op | source)
XLA Modules:
  0.0 83.4 jit_solution(14014912790773999229)
XLA Ops:
  1.3 77.5 %relay.1 = (bf16[256,4096]{1,0:T(8,128)(2,1)}, bf16[256,4096]{1,0:T(8,128)(2,1)}) custom-call(s32[1]{0:T(128)S(6)} %copy.9.valid_ref, bf16[1,2,256,2048]{3,2,1,0:T(8,128)(2,1)} %bitcast.8, bf16[256,4096]{1,0:T(8,128)(2,1)} %bitcast.9, bf16[2048,4096]{1,0:T(8,128)(2,1)} %bitcast.7, f32[1,8192]{1,0:T(1,128)} %gain.1), custom_call_target="tpu_custom_call" | custom-call | flops 17179869184 | bytes 25165824 | tf_op jit(solution)/shard_map/relay/pallas_call | solution.py:299
  78.8 0.0 copy-start
  78.8 3.3 %copy.10 = bf16[1,256,4096]{2,1,0:T(8,128)(2,1)} copy(bf16[1,256,4096]{2,1,0:T(8,128)(2,1)} %bitcast.6) | data formatting | bytes 4194304
  82.0 0.0 copy-done
  82.0 1.3 %copy.11 = bf16[1,256,4096]{2,1,0:T(8,128)(2,1)} copy(bf16[1,256,4096]{2,1,0:T(8,128)(2,1)S(1)} %bitcast.5) | data formatting | bytes 4194304
Async XLA Ops:
  78.8 3.3 %copy-start = (bf16[256,4096]{1,0:T(8,128)(2,1)S(1)}, bf16[256,4096]{1,0:T(8,128)(2,1)}, u32[]{:S(2)}) copy-start(bf16[256,4096]{1,0:T(8,128)(2,1)} %get-tuple-element.5) | copy-start | bytes 6291460

commit v2 on v1

--- a/solution.py
+++ b/solution.py
@@ -11,17 +11,19 @@
 PIECES = 8
 AHEAD = 2
 LAG = 2
+GROUPS = 4
 
 
 def relay_kernel(
     sizes, valid_ref, context, residual, weight, gain, normed, handoff,
-    rows_all, held_w, held_res, mine, pair_out, pair_in, chip_out, chip_in,
+    rows_all, lhs, held_w, held_res, mine, pair_out, pair_in, chip_out, chip_in,
     hidden, passed, scaled, sq_out, sq_in,
     ctx_sem, w_sem, res_sem, y_send, y_recv, pair_send, pair_recv,
     chip_send, chip_recv, z_send, z_recv, sq_send, sq_recv, out_sem, zero_sem,
 ):
     sections, dps, chips, blocks, rows, depth, cols, r, steps, tile = sizes
     tiles = cols // tile
+    half = chips * r
     sec = lax.axis_index("section")
     dp = lax.axis_index("dp")
     tensor = lax.axis_index("tensor")
@@ -38,15 +40,15 @@
     ctx_load = pltpu.make_async_copy(context, rows_all.at[own], ctx_sem)
     ctx_load.start()
 
+    def group(n):
+        return pl.ds(n * tile, tile)
+
     def w_load(n):
-        at = pl.ds(pl.multiple_of(n * tile, tile), tile)
+        at = group(n)
         return pltpu.make_async_copy(weight.at[:, at], held_w.at[:, at], w_sem.at[n])
 
-    def w_start(n, carry):
+    for n in range(tiles):
         w_load(n).start()
-        return carry
-
-    lax.fori_loop(0, tiles, w_start, 0)
     res_load = pltpu.make_async_copy(residual, held_res, res_sem)
     res_load.start()
 
@@ -85,32 +87,32 @@
             device_id_type=MESH,
         )
 
-    def pair_copy(k):
-        return pltpu.make_async_remote_copy(
-            src_ref=pair_out.at[k],
-            dst_ref=pair_in.at[k],
-            send_sem=pair_send.at[k],
-            recv_sem=pair_recv.at[k],
+    def pair_copy(k, n):
+        return pltpu.make_async_remote_copy(
+            src_ref=pair_out.at[k, :, :, group(n)],
+            dst_ref=pair_in.at[k, :, :, group(n)],
+            send_sem=pair_send.at[k, n],
+            recv_sem=pair_recv.at[k, n],
             device_id={"tensor": sibling},
             device_id_type=MESH,
         )
 
-    def chip_copy(k, j):
-        return pltpu.make_async_remote_copy(
-            src_ref=chip_out.at[j, span(k), :],
-            dst_ref=chip_in.at[j, span(k), :],
-            send_sem=chip_send.at[k, j],
-            recv_sem=chip_recv.at[k, j],
+    def chip_copy(k, n, j):
+        return pltpu.make_async_remote_copy(
+            src_ref=chip_out.at[j, span(k), group(n)],
+            dst_ref=chip_in.at[j, span(k), group(n)],
+            send_sem=chip_send.at[k, n, j],
+            recv_sem=chip_recv.at[k, n, j],
             device_id={"tensor": chip_at[j] * 2 + core},
             device_id_type=MESH,
         )
 
-    def z_copy(k):
-        return pltpu.make_async_remote_copy(
-            src_ref=passed.at[span(k), :],
-            dst_ref=handoff.at[span(k), :],
-            send_sem=z_send.at[k],
-            recv_sem=z_recv.at[k],
+    def z_copy(k, n):
+        return pltpu.make_async_remote_copy(
+            src_ref=passed.at[span(k), group(n)],
+            dst_ref=handoff.at[span(k), group(n)],
+            send_sem=z_send.at[k, n],
+            recv_sem=z_recv.at[k, n],
             device_id={"section": lax.rem(sec + 1, sections)},
             device_id_type=MESH,
         )
@@ -155,9 +157,8 @@
         lax.fori_loop(0, steps, finish, 0)
 
     ctx_load.wait()
-    half = chips * r
-
-    def product(k):
+
+    def gather(k):
         for j in range(dps - 1):
             y_copy(k, j).wait_recv()
 
@@ -166,31 +167,30 @@
             for j in range(dps - 1):
                 y_copy(k + AHEAD, j).start()
 
-        def one_tile(n, carry):
-            @pl.when(k == 0)
-            def _():
-                w_load(n).wait()
-
-            at = pl.ds(pl.multiple_of(n * tile, tile), tile)
-            lhs = jnp.concatenate(
-                [rows_all[:, 1 - core, span(k), :], rows_all[:, core, span(k), :]], axis=0
-            ).reshape(2 * half, depth)
-            part = jnp.dot(lhs, held_w[:, at], preferred_element_type=jnp.float32)
-            pair_out[k, :, :, at] = part[:half].astype(jnp.bfloat16).reshape(chips, r, tile)
-            mine[:, :, at] = part[half:].reshape(chips, r, tile)
-            return carry
-
-        lax.fori_loop(0, tiles, one_tile, 0)
-        pair_copy(k).start()
-
-    def combine(k):
-        pair_copy(k).wait_recv()
+        for q in range(chips):
+            lhs[pl.ds(q * r, r), :] = rows_all[q, 1 - core, span(k), :]
+            lhs[pl.ds(half + q * r, r), :] = rows_all[q, core, span(k), :]
+
+    def product(k, n):
+        @pl.when(k == 0)
+        def _():
+            w_load(n).wait()
+
+        part = jnp.dot(lhs[...], held_w[:, group(n)], preferred_element_type=jnp.float32)
+        pair_out[k, :, :, group(n)] = part[:half].astype(jnp.bfloat16).reshape(chips, r, tile)
+        mine[:, :, group(n)] = part[half:].reshape(chips, r, tile)
+        pair_copy(k, n).start()
+
+    def combine(k, n):
+        pair_copy(k, n).wait_recv()
+
+        def pair_sum(q):
+            return mine[q, :, group(n)] + pair_in[k, q, :, group(n)].astype(jnp.float32)
+
         for j in range(chips - 1):
-            both = mine[chip_at[j]] + pair_in[k, chip_at[j]].astype(jnp.float32)
-            chip_out[j, span(k), :] = both.astype(jnp.bfloat16)
-            chip_copy(k, j).start()
-        both = mine[chip] + pair_in[k, chip].astype(jnp.float32)
-        hidden[span(k), :] = both
+            chip_out[j, span(k), group(n)] = pair_sum(chip_at[j]).astype(jnp.bfloat16)
+            chip_copy(k, n, j).start()
+        hidden[span(k), group(n)] = pair_sum(chip)
 
     def row_mask(k):
         ids = tensor * rows + k * r + lax.broadcasted_iota(jnp.int32, (r, 1), 0)
@@ -201,28 +201,29 @@
         def _():
             res_load.wait()
 
-        for j in range(chips - 1):
-            chip_copy(k, j).wait_recv()
         keep = row_mask(k)
         total = jnp.zeros((r, 128), jnp.float32)
         for n in range(tiles):
-            at = pl.ds(n * tile, tile)
+            at = group(n)
+            for j in range(chips - 1):
+                chip_copy(k, n, j).wait_recv()
             h = hidden[span(k), at]
             for j in range(chips - 1):
                 h = h + chip_in[j, span(k), at].astype(jnp.float32)
             h = h + held_res[span(k), at].astype(jnp.float32)
             hidden[span(k), at] = h
             passed[span(k), at] = jnp.where(keep, h, 0.0).astype(jnp.bfloat16)
+
+            @pl.when(sec < sections - 1)
+            def _():
+                z_copy(k, n).start()
+
             sq = h * h
             for c in range(tile // 128):
                 total = total + sq[:, c * 128 : (c + 1) * 128]
         sq_out[k] = total
         for j in range(dps - 1):
             sq_copy(k, j).start()
-
-        @pl.when(sec < sections - 1)
-        def _():
-            z_copy(k).start()
 
     def normalize(k):
         total = sq_out[k]
@@ -240,7 +241,11 @@
     def step(s, carry):
         @pl.when(s < steps)
         def _():
-            product(s)
+            gather(s)
+            product(s, 0)
+            for n in range(1, tiles):
+                product(s, n)
+                combine(s, n - 1)
 
         @pl.when(s > LAG)
         def _():
@@ -248,7 +253,7 @@
 
         @pl.when(s < steps)
         def _():
-            combine(s)
+            combine(s, tiles - 1)
 
         @pl.when((s >= LAG) & (s < steps + LAG))
         def _():
@@ -262,18 +267,21 @@
         for j in range(dps - 1):
             y_copy(k, j).wait_send()
             sq_copy(k, j).wait_send()
-        pair_copy(k).wait_send()
-        for j in range(chips - 1):
-            chip_copy(k, j).wait_send()
         out_copy(k).wait()
+        for n in range(tiles):
+            pair_copy(k, n).wait_send()
+            for j in range(chips - 1):
+                chip_copy(k, n, j).wait_send()
 
         @pl.when(sec < sections - 1)
         def _():
-            z_copy(k).wait_send()
+            for n in range(tiles):
+                z_copy(k, n).wait_send()
 
         @pl.when(sec > 0)
         def _():
-            z_copy(k).wait_recv()
+            for n in range(tiles):
+                z_copy(k, n).wait_recv()
 
         return carry
 
@@ -289,7 +297,8 @@
     assert blocks * dps == chips
     r = max(16, rows // PIECES)
     steps = rows // r
-    tile = min(512, cols)
+    tile = cols // GROUPS
+    tiles = GROUPS
     sizes = (sections, dps, chips, blocks, rows, depth, cols, r, steps, tile)
     bf16, f32 = jnp.bfloat16, jnp.float32
     dma = pltpu.SemaphoreType.DMA
@@ -309,6 +318,7 @@
         out_specs=(anywhere, anywhere),
         scratch_shapes=[
             pltpu.VMEM((chips, 2, rows, depth), bf16),
+            pltpu.VMEM((2 * chips * r, depth), bf16),
             pltpu.VMEM((depth, cols), bf16),
             pltpu.VMEM((rows, cols), bf16),
             pltpu.VMEM((chips, r, cols), f32),
@@ -322,16 +332,16 @@
             pltpu.VMEM((steps, r, 128), f32),
             pltpu.VMEM((dps - 1, steps, r, 128), f32),
             dma,
-            dma((cols // tile,)),
+            dma((tiles,)),
             dma,
             dma((steps, dps - 1)),
             dma((steps, dps - 1)),
-            dma((steps,)),
-            dma((steps,)),
-            dma((steps, chips - 1)),
-            dma((steps, chips - 1)),
-            dma((steps,)),
-            dma((steps,)),
+            dma((steps, tiles)),
+            dma((steps, tiles)),
+            dma((steps, tiles, chips - 1)),
+            dma((steps, tiles, chips - 1)),
+            dma((steps, tiles)),
+            dma((steps, tiles)),
             dma((steps, dps - 1)),
             dma((steps, dps - 1)),
             dma((steps,)),

time: 83.6 us -> 83.4 us (level)
  no operation moved by 1% of the time
where the time goes in v2:
time: 83.4 us; the launch traced here: 83.2 us
  Pallas kernels  77.3 us (93%)
  local copies, waits for them, and re-layouts  4.6 us (6%)
  between operations  1.29 us (2%)
    pallas_call x1, Pallas kernels, on_device(): pl.pallas_call(functools.partial(relay_kernel, sizes), out_shape=(out, ou...  77.3 us
    unnamed x4, local copies, waits for them, and re-layouts  4.6 us

profile of v2, /device:TPU:0, one launch (start us, length us, event | category | flops | bytes accessed | tf_op | source)
XLA Modules:
  0.0 83.2 jit_solution(2043038466371782193)
XLA Ops:
  1.3 77.3 %relay.1 = (bf16[256,4096]{1,0:T(8,128)(2,1)}, bf16[256,4096]{1,0:T(8,128)(2,1)}) custom-call(s32[1]{0:T(128)S(6)} %copy.9.valid_ref, bf16[1,2,256,2048]{3,2,1,0:T(8,128)(2,1)} %bitcast.8, bf16[256,4096]{1,0:T(8,128)(2,1)} %bitcast.9, bf16[2048,4096]{1,0:T(8,128)(2,1)} %bitcast.7, f32[1,8192]{1,0:T(1,128)} %gain.1), custom_call_target="tpu_custom_call" | custom-call | flops 17179869184 | bytes 25165824 | tf_op jit(solution)/shard_map/relay/pallas_call | solution.py:308
  78.6 0.0 copy-start
  78.6 3.3 %copy.10 = bf16[1,256,4096]{2,1,0:T(8,128)(2,1)} copy(bf16[1,256,4096]{2,1,0:T(8,128)(2,1)} %bitcast.6) | data formatting | bytes 4194304
  81.9 0.0 copy-done
  81.9 1.3 %copy.11 = bf16[1,256,4096]{2,1,0:T(8,128)(2,1)} copy(bf16[1,256,4096]{2,1,0:T(8,128)(2,1)S(1)} %bitcast.5) | data formatting | bytes 4194304
Async XLA Ops:
  78.6 3.3 %copy-start = (bf16[256,4096]{1,0:T(8,128)(2,1)S(1)}, bf16[256,4096]{1,0:T(8,128)(2,1)}, u32[]{:S(2)}) copy-start(bf16[256,4096]{1,0:T(8,128)(2,1)} %get-tuple-element.5) | copy-start | bytes 6291460

commit v3 on v2

--- a/solution.py
+++ b/solution.py
@@ -9,8 +9,6 @@
 
 MESH = pl.DeviceIdType.MESH
 PIECES = 8
-AHEAD = 2
-LAG = 2
 GROUPS = 4
 
 
@@ -137,9 +135,11 @@
             passed.at[span(0), :], handoff.at[span(k), :], zero_sem.at[k]
         )
 
-    for k in range(min(AHEAD, steps)):
+    def y_start(k):
         for j in range(dps - 1):
             y_copy(k, j).start()
+
+    y_start(0)
 
     @pl.when(sec == 0)
     def _():
@@ -156,16 +156,15 @@
         lax.fori_loop(0, steps, begin, 0)
         lax.fori_loop(0, steps, finish, 0)
 
+    for j in range(dps - 1):
+        y_copy(0, j).wait_send()
+    if steps > 1:
+        y_start(1)
     ctx_load.wait()
 
     def gather(k):
         for j in range(dps - 1):
             y_copy(k, j).wait_recv()
-
-        @pl.when(k + AHEAD < steps)
-        def _():
-            for j in range(dps - 1):
-                y_copy(k + AHEAD, j).start()
 
         for q in range(chips):
             lhs[pl.ds(q * r, r), :] = rows_all[q, 1 - core, span(k), :]
@@ -196,34 +195,35 @@
         ids = tensor * rows + k * r + lax.broadcasted_iota(jnp.int32, (r, 1), 0)
         return ids < valid_ref[0]
 
-    def add_residual(k):
-        @pl.when(k == 0)
-        def _():
-            res_load.wait()
-
-        keep = row_mask(k)
-        total = jnp.zeros((r, 128), jnp.float32)
-        for n in range(tiles):
-            at = group(n)
-            for j in range(chips - 1):
-                chip_copy(k, n, j).wait_recv()
-            h = hidden[span(k), at]
-            for j in range(chips - 1):
-                h = h + chip_in[j, span(k), at].astype(jnp.float32)
-            h = h + held_res[span(k), at].astype(jnp.float32)
-            hidden[span(k), at] = h
-            passed[span(k), at] = jnp.where(keep, h, 0.0).astype(jnp.bfloat16)
-
-            @pl.when(sec < sections - 1)
+    def add_residual(k, n):
+        if n == 0:
+
+            @pl.when(k == 0)
             def _():
-                z_copy(k, n).start()
-
-            sq = h * h
-            for c in range(tile // 128):
-                total = total + sq[:, c * 128 : (c + 1) * 128]
-        sq_out[k] = total
-        for j in range(dps - 1):
-            sq_copy(k, j).start()
+                res_load.wait()
+
+        at = group(n)
+        for j in range(chips - 1):
+            chip_copy(k, n, j).wait_recv()
+        h = hidden[span(k), at]
+        for j in range(chips - 1):
+            h = h + chip_in[j, span(k), at].astype(jnp.float32)
+        h = h + held_res[span(k), at].astype(jnp.float32)
+        hidden[span(k), at] = h
+        passed[span(k), at] = jnp.where(row_mask(k), h, 0.0).astype(jnp.bfloat16)
+
+        @pl.when(sec < sections - 1)
+        def _():
+            z_copy(k, n).start()
+
+        sq = h * h
+        total = sq[:, :128]
+        for c in range(1, tile // 128):
+            total = total + sq[:, c * 128 : (c + 1) * 128]
+        sq_out[k] = total if n == 0 else sq_out[k] + total
+        if n == tiles - 1:
+            for j in range(dps - 1):
+                sq_copy(k, j).start()
 
     def normalize(k):
         total = sq_out[k]
@@ -242,30 +242,47 @@
         @pl.when(s < steps)
         def _():
             gather(s)
-            product(s, 0)
-            for n in range(1, tiles):
+
+        for n in range(tiles):
+
+            @pl.when(s < steps)
+            def _():
                 product(s, n)
-                combine(s, n - 1)
-
-        @pl.when(s > LAG)
-        def _():
-            normalize(s - LAG - 1)
+                if n > 0:
+                    combine(s, n - 1)
+
+            if n == max(0, tiles - 2):
+
+                @pl.when(s + 2 < steps)
+                def _():
+                    y_start(s + 2)
+
+            if n > 0:
+
+                @pl.when((s > 0) & (s <= steps))
+                def _():
+                    add_residual(s - 1, n)
 
         @pl.when(s < steps)
         def _():
             combine(s, tiles - 1)
-
-        @pl.when((s >= LAG) & (s < steps + LAG))
-        def _():
-            add_residual(s - LAG)
+            add_residual(s, 0)
+
+        @pl.when(s > 1)
+        def _():
+            normalize(s - 2)
 
         return carry
 
-    lax.fori_loop(0, steps + LAG + 1, step, 0)
+    lax.fori_loop(0, steps + 2, step, 0)
 
     def drain(k, carry):
+        @pl.when(k > 0)
+        def _():
+            for j in range(dps - 1):
+                y_copy(k, j).wait_send()
+
         for j in range(dps - 1):
-            y_copy(k, j).wait_send()
             sq_copy(k, j).wait_send()
         out_copy(k).wait()
         for n in range(tiles):

time: 83.4 us -> 75 us (0.90)
  Pallas kernels: 77.3 us -> 68.9 us
    pallas_call x1, Pallas kernels: 77.3 us -> 68.9 us  [on_device(): pl.pallas_call(functools.partial(relay_kernel, sizes), out_shape=(out, ou...]
where the time goes in v3:
time: 75 us; the launch traced here: 74.8 us
  Pallas kernels  68.9 us (92%)
  local copies, waits for them, and re-layouts  4.6 us (6%)
  between operations  1.29 us (2%)
    pallas_call x1, Pallas kernels, on_device(): pl.pallas_call(functools.partial(relay_kernel, sizes), out_shape=(out, ou...  68.9 us
    unnamed x4, local copies, waits for them, and re-layouts  4.6 us

profile of v3, /device:TPU:0, one launch (start us, length us, event | category | flops | bytes accessed | tf_op | source)
XLA Modules:
  0.0 74.8 jit_solution(16894617827651083499)
XLA Ops:
  1.3 68.9 %relay.1 = (bf16[256,4096]{1,0:T(8,128)(2,1)}, bf16[256,4096]{1,0:T(8,128)(2,1)}) custom-call(s32[1]{0:T(128)S(6)} %copy.9.valid_ref, bf16[1,2,256,2048]{3,2,1,0:T(8,128)(2,1)} %bitcast.8, bf16[256,4096]{1,0:T(8,128)(2,1)} %bitcast.9, bf16[2048,4096]{1,0:T(8,128)(2,1)} %bitcast.7, f32[1,8192]{1,0:T(1,128)} %gain.1), custom_call_target="tpu_custom_call" | custom-call | flops 17179869184 | bytes 25165824 | tf_op jit(solution)/shard_map/relay/pallas_call | solution.py:325
  70.2 0.0 copy-start
  70.2 3.3 %copy.10 = bf16[1,256,4096]{2,1,0:T(8,128)(2,1)} copy(bf16[1,256,4096]{2,1,0:T(8,128)(2,1)} %bitcast.6) | data formatting | bytes 4194304
  73.5 0.0 copy-done
  73.5 1.3 %copy.11 = bf16[1,256,4096]{2,1,0:T(8,128)(2,1)} copy(bf16[1,256,4096]{2,1,0:T(8,128)(2,1)S(1)} %bitcast.5) | data formatting | bytes 4194304
Async XLA Ops:
  70.2 3.3 %copy-start = (bf16[256,4096]{1,0:T(8,128)(2,1)S(1)}, bf16[256,4096]{1,0:T(8,128)(2,1)}, u32[]{:S(2)}) copy-start(bf16[256,4096]{1,0:T(8,128)(2,1)} %get-tuple-element.5) | copy-start | bytes 6291460

commit v4 on v3

--- a/solution.py
+++ b/solution.py
@@ -15,13 +15,14 @@
 def relay_kernel(
     sizes, valid_ref, context, residual, weight, gain, normed, handoff,
     rows_all, lhs, held_w, held_res, mine, pair_out, pair_in, chip_out, chip_in,
-    hidden, passed, scaled, sq_out, sq_in,
+    hidden, passed, sq_out, sq_in,
     ctx_sem, w_sem, res_sem, y_send, y_recv, pair_send, pair_recv,
-    chip_send, chip_recv, z_send, z_recv, sq_send, sq_recv, out_sem, zero_sem,
+    chip_send, chip_recv, z_send, z_recv, sq_send, sq_recv,
 ):
     sections, dps, chips, blocks, rows, depth, cols, r, steps, tile = sizes
     tiles = cols // tile
     half = chips * r
+    first = (tiles + 1) // 2
     sec = lax.axis_index("section")
     dp = lax.axis_index("dp")
     tensor = lax.axis_index("tensor")
@@ -125,42 +126,25 @@
             device_id_type=MESH,
         )
 
-    def out_copy(k):
-        return pltpu.make_async_copy(
-            scaled.at[span(k), :], normed.at[span(k), :], out_sem.at[k]
-        )
-
-    def zero_copy(k):
-        return pltpu.make_async_copy(
-            passed.at[span(0), :], handoff.at[span(k), :], zero_sem.at[k]
-        )
-
     def y_start(k):
         for j in range(dps - 1):
             y_copy(k, j).start()
 
     y_start(0)
-
-    @pl.when(sec == 0)
-    def _():
-        passed[span(0), :] = jnp.zeros((r, cols), passed.dtype)
-
-        def begin(k, carry):
-            zero_copy(k).start()
-            return carry
-
-        def finish(k, carry):
-            zero_copy(k).wait()
-            return carry
-
-        lax.fori_loop(0, steps, begin, 0)
-        lax.fori_loop(0, steps, finish, 0)
 
     for j in range(dps - 1):
         y_copy(0, j).wait_send()
     if steps > 1:
         y_start(1)
     ctx_load.wait()
+
+    @pl.when(sec == 0)
+    def _():
+        def clear(k, carry):
+            handoff[span(k), :] = jnp.zeros((r, cols), handoff.dtype)
+            return carry
+
+        lax.fori_loop(0, steps, clear, 0)
 
     def gather(k):
         for j in range(dps - 1):
@@ -235,8 +219,7 @@
         for n in range(tiles):
             at = pl.ds(n * tile, tile)
             g = gain[:, pl.ds(pl.multiple_of(dp * cols + n * tile, tile), tile)]
-            scaled[span(k), at] = (hidden[span(k), at] * scale * g).astype(jnp.bfloat16)
-        out_copy(k).start()
+            normed[span(k), at] = (hidden[span(k), at] * scale * g).astype(jnp.bfloat16)
 
     def step(s, carry):
         @pl.when(s < steps)
@@ -257,16 +240,17 @@
                 def _():
                     y_start(s + 2)
 
-            if n > 0:
+            if n + first < tiles:
 
                 @pl.when((s > 0) & (s <= steps))
                 def _():
-                    add_residual(s - 1, n)
+                    add_residual(s - 1, n + first)
 
         @pl.when(s < steps)
         def _():
             combine(s, tiles - 1)
-            add_residual(s, 0)
+            for n in range(first):
+                add_residual(s, n)
 
         @pl.when(s > 1)
         def _():
@@ -284,7 +268,6 @@
 
         for j in range(dps - 1):
             sq_copy(k, j).wait_send()
-        out_copy(k).wait()
         for n in range(tiles):
             pair_copy(k, n).wait_send()
             for j in range(chips - 1):
@@ -321,7 +304,7 @@
     dma = pltpu.SemaphoreType.DMA
     total_rows = local * dps
     anywhere = pl.BlockSpec(memory_space=pl.ANY)
-    out = jax.ShapeDtypeStruct((rows, cols), bf16)
+    out = pltpu.VMEM((rows, cols), bf16)
     normed, handoff = pl.pallas_call(
         functools.partial(relay_kernel, sizes),
         out_shape=(out, out),
@@ -332,7 +315,7 @@
             anywhere,
             pl.BlockSpec(memory_space=pltpu.VMEM),
         ],
-        out_specs=(anywhere, anywhere),
+        out_specs=(pl.BlockSpec(memory_space=pltpu.VMEM),) * 2,
         scratch_shapes=[
             pltpu.VMEM((chips, 2, rows, depth), bf16),
             pltpu.VMEM((2 * chips * r, depth), bf16),
@@ -344,7 +327,6 @@
             pltpu.VMEM((chips - 1, rows, cols), bf16),
             pltpu.VMEM((chips - 1, rows, cols), bf16),
             pltpu.VMEM((rows, cols), f32),
-            pltpu.VMEM((rows, cols), bf16),
             pltpu.VMEM((rows, cols), bf16),
             pltpu.VMEM((steps, r, 128), f32),
             pltpu.VMEM((dps - 1, steps, r, 128), f32),
@@ -361,8 +343,6 @@
             dma((steps, tiles)),
             dma((steps, dps - 1)),
             dma((steps, dps - 1)),
-            dma((steps,)),
-            dma((steps,)),
         ],
         compiler_params=pltpu.CompilerParams(
             collective_id=0, has_side_effects=True, vmem_limit_bytes=56 * 2**20

time: 75 us -> 80.3 us (1.071)
  Pallas kernels: 68.9 us -> 76.2 us
  local copies, waits for them, and re-layouts: 4.6 us -> 2.64 us
    pallas_call x1, Pallas kernels: 68.9 us -> 76.2 us  [on_device(): pl.pallas_call(functools.partial(relay_kernel, sizes), out_shape=(out, ou...]
    unnamed x4 -> x2, local copies, waits for them, and re-layouts: 4.6 us -> 2.64 us
where the time goes in v4:
time: 80.3 us; the launch traced here: 80.1 us
  Pallas kernels  76.2 us (95%)
  local copies, waits for them, and re-layouts  2.64 us (3%)
  between operations  1.29 us (2%)
    pallas_call x1, Pallas kernels, on_device(): pl.pallas_call(functools.partial(relay_kernel, sizes), out_shape=(out, ou...  76.2 us
    unnamed x2, local copies, waits for them, and re-layouts  2.64 us

profile of v4, /device:TPU:0, one launch (start us, length us, event | category | flops | bytes accessed | tf_op | source)
XLA Modules:
  0.0 80.1 jit_solution(12500162788229913587)
XLA Ops:
  1.3 76.2 %relay.1 = (bf16[256,4096]{1,0:T(8,128)(2,1)S(1)}, bf16[256,4096]{1,0:T(8,128)(2,1)S(1)}) custom-call(s32[1]{0:T(128)S(6)} %copy.11.valid_ref, bf16[1,2,256,2048]{3,2,1,0:T(8,128)(2,1)} %bitcast.8, bf16[256,4096]{1,0:T(8,128)(2,1)} %bitcast.9, bf16[2048,4096]{1,0:T(8,128)(2,1)} %bitcast.7, f32[1,8192]{1,0:T(1,128)} %gain.1), custom_call_target="tpu_custom_call" | custom-call | flops 17179869184 | bytes 25165824 | tf_op jit(solution)/shard_map/relay/pallas_call | solution.py:308
  77.5 1.3 %copy.9 = bf16[1,256,4096]{2,1,0:T(8,128)(2,1)} copy(bf16[1,256,4096]{2,1,0:T(8,128)(2,1)S(1)} %bitcast.6) | data formatting | bytes 4194304
  78.8 1.3 %copy.10 = bf16[1,256,4096]{2,1,0:T(8,128)(2,1)} copy(bf16[1,256,4096]{2,1,0:T(8,128)(2,1)S(1)} %bitcast.5) | data formatting | bytes 4194304

commit v5 on v4

--- a/solution.py
+++ b/solution.py
@@ -22,7 +22,6 @@
     sections, dps, chips, blocks, rows, depth, cols, r, steps, tile = sizes
     tiles = cols // tile
     half = chips * r
-    first = (tiles + 1) // 2
     sec = lax.axis_index("section")
     dp = lax.axis_index("dp")
     tensor = lax.axis_index("tensor")
@@ -234,23 +233,21 @@
                 if n > 0:
                     combine(s, n - 1)
 
+            if n == 0:
+
+                @pl.when((s > 0) & (s <= steps))
+                def _():
+                    combine(s - 1, tiles - 1)
+
             if n == max(0, tiles - 2):
 
                 @pl.when(s + 2 < steps)
                 def _():
                     y_start(s + 2)
 
-            if n + first < tiles:
-
-                @pl.when((s > 0) & (s <= steps))
-                def _():
-                    add_residual(s - 1, n + first)
-
-        @pl.when(s < steps)
-        def _():
-            combine(s, tiles - 1)
-            for n in range(first):
-                add_residual(s, n)
+            @pl.when((s > 0) & (s <= steps))
+            def _():
+                add_residual(s - 1, n)
 
         @pl.when(s > 1)
         def _():

time: 80.3 us -> 72.4 us (0.902)
  Pallas kernels: 76.2 us -> 68.3 us
    pallas_call x1, Pallas kernels: 76.2 us -> 68.3 us  [on_device(): pl.pallas_call(functools.partial(relay_kernel, sizes), out_shape=(out, ou...]
where the time goes in v5:
time: 72.4 us; the launch traced here: 72.2 us
  Pallas kernels  68.3 us (94%)
  local copies, waits for them, and re-layouts  2.64 us (4%)
  between operations  1.29 us (2%)
    pallas_call x1, Pallas kernels, on_device(): pl.pallas_call(functools.partial(relay_kernel, sizes), out_shape=(out, ou...  68.3 us
    unnamed x2, local copies, waits for them, and re-layouts  2.64 us

profile of v5, /device:TPU:0, one launch (start us, length us, event | category | flops | bytes accessed | tf_op | source)
XLA Modules:
  0.0 72.2 jit_solution(18029478103483352347)
XLA Ops:
  1.3 68.3 %relay.1 = (bf16[256,4096]{1,0:T(8,128)(2,1)S(1)}, bf16[256,4096]{1,0:T(8,128)(2,1)S(1)}) custom-call(s32[1]{0:T(128)S(6)} %copy.11.valid_ref, bf16[1,2,256,2048]{3,2,1,0:T(8,128)(2,1)} %bitcast.8, bf16[256,4096]{1,0:T(8,128)(2,1)} %bitcast.9, bf16[2048,4096]{1,0:T(8,128)(2,1)} %bitcast.7, f32[1,8192]{1,0:T(1,128)} %gain.1), custom_call_target="tpu_custom_call" | custom-call | flops 17179869184 | bytes 25165824 | tf_op jit(solution)/shard_map/relay/pallas_call | solution.py:305
  69.5 1.3 %copy.9 = bf16[1,256,4096]{2,1,0:T(8,128)(2,1)} copy(bf16[1,256,4096]{2,1,0:T(8,128)(2,1)S(1)} %bitcast.6) | data formatting | bytes 4194304
  70.9 1.3 %copy.10 = bf16[1,256,4096]{2,1,0:T(8,128)(2,1)} copy(bf16[1,256,4096]{2,1,0:T(8,128)(2,1)S(1)} %bitcast.5) | data formatting | bytes 4194304

commit v6 on v5

--- a/solution.py
+++ b/solution.py
@@ -8,8 +8,8 @@
 from jax.sharding import PartitionSpec as P
 
 MESH = pl.DeviceIdType.MESH
-PIECES = 8
-GROUPS = 4
+PIECES = 16
+GROUPS = 2
 
 
 def relay_kernel(
@@ -149,6 +149,10 @@
         for j in range(dps - 1):
             y_copy(k, j).wait_recv()
 
+        @pl.when(k + 2 < steps)
+        def _():
+            y_start(k + 2)
+
         for q in range(chips):
             lhs[pl.ds(q * r, r), :] = rows_all[q, 1 - core, span(k), :]
             lhs[pl.ds(half + q * r, r), :] = rows_all[q, core, span(k), :]
@@ -238,12 +242,6 @@
                 @pl.when((s > 0) & (s <= steps))
                 def _():
                     combine(s - 1, tiles - 1)
-
-            if n == max(0, tiles - 2):
-
-                @pl.when(s + 2 < steps)
-                def _():
-                    y_start(s + 2)
 
             @pl.when((s > 0) & (s <= steps))
             def _():

time: 72.4 us -> 102 us (1.41)
  Pallas kernels: 68.3 us -> 97.8 us
    pallas_call x1, Pallas kernels: 68.3 us -> 97.8 us  [on_device(): pl.pallas_call(functools.partial(relay_kernel, sizes), out_shape=(out, ou...]
where the time goes in v6:
time: 102 us
  Pallas kernels  97.8 us (96%)
  local copies, waits for them, and re-layouts  2.64 us (3%)
  between operations  1.29 us (1%)
    pallas_call x1, Pallas kernels, on_device(): pl.pallas_call(functools.partial(relay_kernel, sizes), out_shape=(out, ou...  97.8 us
    unnamed x2, local copies, waits for them, and re-layouts  2.64 us

profile of v6, /device:TPU:0, one launch (start us, length us, event | category | flops | bytes accessed | tf_op | source)
XLA Modules:
  0.0 101.7 jit_solution(11026372467180592657)
XLA Ops:
  1.3 97.8 %relay.1 = (bf16[256,4096]{1,0:T(8,128)(2,1)S(1)}, bf16[256,4096]{1,0:T(8,128)(2,1)S(1)}) custom-call(s32[1]{0:T(128)S(6)} %copy.11.valid_ref, bf16[1,2,256,2048]{3,2,1,0:T(8,128)(2,1)} %bitcast.8, bf16[256,4096]{1,0:T(8,128)(2,1)} %bitcast.9, bf16[2048,4096]{1,0:T(8,128)(2,1)} %bitcast.7, f32[1,8192]{1,0:T(1,128)} %gain.1), custom_call_target="tpu_custom_call" | custom-call | flops 17179869184 | bytes 25165824 | tf_op jit(solution)/shard_map/relay/pallas_call | solution.py:303
  99.1 1.3 %copy.9 = bf16[1,256,4096]{2,1,0:T(8,128)(2,1)} copy(bf16[1,256,4096]{2,1,0:T(8,128)(2,1)S(1)} %bitcast.6) | data formatting | bytes 4194304
  100.4 1.3 %copy.10 = bf16[1,256,4096]{2,1,0:T(8,128)(2,1)} copy(bf16[1,256,4096]{2,1,0:T(8,128)(2,1)S(1)} %bitcast.5) | data formatting | bytes 4194304

commit v7 on v6

--- a/solution.py
+++ b/solution.py
@@ -8,8 +8,8 @@
 from jax.sharding import PartitionSpec as P
 
 MESH = pl.DeviceIdType.MESH
-PIECES = 16
-GROUPS = 2
+PIECES = 8
+GROUPS = 4
 
 
 def relay_kernel(
@@ -247,13 +247,15 @@
             def _():
                 add_residual(s - 1, n)
 
-        @pl.when(s > 1)
-        def _():
-            normalize(s - 2)
-
         return carry
 
-    lax.fori_loop(0, steps + 2, step, 0)
+    lax.fori_loop(0, steps + 1, step, 0)
+
+    def finish(k, carry):
+        normalize(k)
+        return carry
+
+    lax.fori_loop(0, steps, finish, 0)
 
     def drain(k, carry):
         @pl.when(k > 0)

time: 102 us -> 72.5 us (0.71)
  Pallas kernels: 97.8 us -> 68.4 us
    pallas_call x1, Pallas kernels: 97.8 us -> 68.4 us  [on_device(): pl.pallas_call(functools.partial(relay_kernel, sizes), out_shape=(out, ou...]
where the time goes in v7:
time: 72.5 us; the launch traced here: 72.3 us
  Pallas kernels  68.4 us (94%)
  local copies, waits for them, and re-layouts  2.64 us (4%)
  between operations  1.29 us (2%)
    pallas_call x1, Pallas kernels, on_device(): pl.pallas_call(functools.partial(relay_kernel, sizes), out_shape=(out, ou...  68.4 us
    unnamed x2, local copies, waits for them, and re-layouts  2.64 us

profile of v7, /device:TPU:0, one launch (start us, length us, event | category | flops | bytes accessed | tf_op | source)
XLA Modules:
  0.0 72.3 jit_solution(7615196015063020984)
XLA Ops:
  1.3 68.4 %relay.1 = (bf16[256,4096]{1,0:T(8,128)(2,1)S(1)}, bf16[256,4096]{1,0:T(8,128)(2,1)S(1)}) custom-call(s32[1]{0:T(128)S(6)} %copy.11.valid_ref, bf16[1,2,256,2048]{3,2,1,0:T(8,128)(2,1)} %bitcast.8, bf16[256,4096]{1,0:T(8,128)(2,1)} %bitcast.9, bf16[2048,4096]{1,0:T(8,128)(2,1)} %bitcast.7, f32[1,8192]{1,0:T(1,128)} %gain.1), custom_call_target="tpu_custom_call" | custom-call | flops 17179869184 | bytes 25165824 | tf_op jit(solution)/shard_map/relay/pallas_call | solution.py:305
  69.7 1.3 %copy.9 = bf16[1,256,4096]{2,1,0:T(8,128)(2,1)} copy(bf16[1,256,4096]{2,1,0:T(8,128)(2,1)S(1)} %bitcast.6) | data formatting | bytes 4194304
  71.0 1.3 %copy.10 = bf16[1,256,4096]{2,1,0:T(8,128)(2,1)} copy(bf16[1,256,4096]{2,1,0:T(8,128)(2,1)S(1)} %bitcast.5) | data formatting | bytes 4194304
